TPU v7x, 512 devices: a whole 4x4x16 slice. The times are simulated.
512 devices in a mesh: sup: 64 (over z, y), cls: 8 (over x, core).
Axes of the slice: x: 4, y: 4, z: 16, core: 2. Of those that a mesh axis runs over, the one named last changes fastest.
Arguments:
- support_feats: bfloat16 [2048, 8192], P('sup', 'cls'), may hold values from -6 to 6
- target_feats: bfloat16 [512, 8192], P('sup', 'cls'), may hold values from -6 to 6
- scales: bfloat16 [2048], replicated, may hold values from 0.5 to 2
- soft_labels: float32 [2048, 21504], P('sup', 'cls'), may hold values from -6 to 6
- target_labels: int32 [512], P('sup'), may hold values from 0 to 21503
Outputs:
- predictions: bfloat16 [512, 21504], P('sup', 'cls')
- hypergrad: float32 [2048, 21504], P('sup', 'cls')
All inputs are finite; a program needn't handle non-finite values.
Results may differ from a plain program's by a relative error of at most 0.017.
Values may be sent and summed in bfloat16 or wider, within the bound.
A program may use at most 64 MiB of HBM per device.

v0:
```python
import jax
import jax.numpy as jnp
from jax import lax
from jax.sharding import PartitionSpec as P

F = 8192
ITERS = 2


RIDGE = 0.05
LABEL_SCALE = 16.0


def conjugate(rhs, kernel):
    result = jnp.zeros_like(rhs)
    resid = rhs
    direction = rhs
    norm_now = jnp.sum(resid * resid, axis=0)
    for step in range(ITERS):
        image = jnp.dot(kernel, direction.astype(jnp.bfloat16), preferred_element_type=jnp.float32)
        curve = jnp.sum(direction * image, axis=0)
        step_size = norm_now / curve
        result = result + step_size * direction
        resid = resid - step_size * image
        norm_next = jnp.sum(resid * resid, axis=0)
        direction = resid + norm_next / norm_now * direction
        norm_now = norm_next
    return result


def local(support_feats, target_feats, scales, soft_labels, target_labels):
    own_support = support_feats.shape[0]
    own_targets = target_feats.shape[0]
    class_count = soft_labels.shape[1]
    sup_count = lax.axis_size("sup")
    support_total = own_support * sup_count
    block_rows = own_targets + own_support
    scale_vec = scales.astype(jnp.float32)
    sup_index = lax.axis_index("sup")
    support_first = sup_index * own_support
    local_rows = jnp.concatenate([target_feats, support_feats], axis=0)
    partial_gram = lax.dot_general(
        local_rows,
        lax.all_gather(support_feats, "sup", axis=0, tiled=True),
        (((1,), (1,)), ((), ())),
        preferred_element_type=jnp.float32,
    )
    own_scales = lax.dynamic_slice_in_dim(scale_vec, support_first, own_support)
    factor_all = jnp.concatenate([jnp.ones((own_targets,), jnp.float32), own_scales])
    summed = lax.psum(partial_gram, "cls")
    count = summed.shape[0]
    rows = lax.iota(jnp.int32, count)
    support_index = support_first + rows - own_targets
    on_diag = (lax.iota(jnp.int32, support_total)[None, :] == support_index[:, None]) & (
        rows >= own_targets
    )[:, None]
    scaled = summed * (factor_all[:, None] * scale_vec[None, :]) / F
    kernels = lax.all_gather(
        (scaled + jnp.where(on_diag, RIDGE, 0.0)).astype(jnp.bfloat16), "sup", axis=0, tiled=True
    )
    blocks = kernels.reshape(sup_count, block_rows, support_total)
    cross_kernel = blocks[:, :own_targets].reshape(sup_count * own_targets, support_total)
    support_kernel = blocks[:, own_targets:].reshape(support_total, support_total)
    label_cols = lax.all_to_all(soft_labels, "sup", split_axis=1, concat_axis=0, tiled=True)
    col_width = label_cols.shape[1]
    labels_all = lax.all_gather(target_labels, "sup", axis=0, tiled=True)
    columns = (
        lax.axis_index("cls") * class_count + sup_index * col_width + lax.iota(jnp.int32, col_width)
    )
    alpha = conjugate(label_cols, support_kernel)
    predicted = jnp.dot(
        cross_kernel, alpha.astype(jnp.bfloat16), preferred_element_type=jnp.float32
    )
    onehot = (labels_all[:, None] == columns[None, :]).astype(jnp.float32)
    misfit = (predicted - LABEL_SCALE * onehot).astype(jnp.bfloat16)
    rhs = lax.dot_general(
        cross_kernel, misfit, (((0,), (0,)), ((), ())), preferred_element_type=jnp.float32
    )
    hyper_cols = conjugate(rhs, support_kernel)
    predictions = lax.all_to_all(
        predicted.astype(jnp.bfloat16), "sup", split_axis=0, concat_axis=1, tiled=True
    )
    hypergrad = lax.all_to_all(hyper_cols, "sup", split_axis=0, concat_axis=1, tiled=True)
    return (predictions, hypergrad)


def solution(mesh):
    in_specs = (P("sup", "cls"), P("sup", "cls"), P(), P("sup", "cls"), P("sup"))
    out_specs = (P("sup", "cls"), P("sup", "cls"))
    return jax.shard_map(local, mesh=mesh, in_specs=in_specs, out_specs=out_specs, check_vma=False)
```

profile of v0, /device:TPU:1, one launch (start us, length us, event | category | flops | bytes accessed | tf_op | source)
XLA Modules:
  0.0 495.9 jit_solution(16016471179538416669)
XLA Ops:
  8.0 146.8 %all-gather.3.cloned.1.call-done = bf16[2048,1024]{1,0:T(8,128)(2,1)} async-done(((bf16[32,1024]{1,0:T(8,128)(2,1)}), bf16[2048,1024]{1,0:T(8,128)(2,1)}) %all-gather.3.cloned.1.call-update) | async-done | bytes 4194320 | tf_op jit(solution)/shard_map/all_gather | solution.py:44
  154.8 4.3 fusion.17
  160.7 75.4 %all-reduce.4.cloned.1.call-done = f32[40,2048]{1,0:T(8,128)} async-done(((f32[40,2048]{1,0:T(8,128)}), f32[40,2048]{1,0:T(8,128)}) %all-reduce.4.cloned.1.call-update) | async-done | bytes 327696 | tf_op jit(solution)/shard_map/psum | solution.py:50
  236.1 1.8 add_convert_fusion.1
  238.0 2.3 all_to_all.42
  240.9 2.2 reshape.77
  243.1 14.7 %all-to-all-start = ((f32[64,1,1344]{2,1,0:T(1,128)}), f32[64,1,1344]{2,1,0:T(1,128)S(1)}, u32[]{:S(2)}, u32[]{:S(2)}) async-start(f32[64,1,1344]{2,1,0:T(1,128)} %reshape.77), calls=%async_computation | async-start | bytes 720896 | tf_op jit(solution)/shard_map/all_to_all | solution.py:64
  260.0 30.8 %all-reduce.1 = s32[512]{0:T(512)S(1)} all-reduce(s32[512]{0:T(512)S(1)} %dynamic-update-slice), channel_id=1, replica_groups=mesh['sup'=64,'cls'=8] {'sup'}, use_global_device_ids=true, to_apply=%add.1 | all-reduce | flops 512 | bytes 4096
  291.4 1.5 reduce.1
  292.8 1.4 reshape.78
  297.2 106.6 %all-gather.5.cloned.1.call-done = bf16[2560,2048]{1,0:T(8,128)(2,1)} async-done(((bf16[40,2048]{1,0:T(8,128)(2,1)}), bf16[2560,2048]{1,0:T(8,128)(2,1)}) %all-gather.5.cloned.1.call-update) | async-done | bytes 10485776 | tf_op jit(solution)/shard_map/all_gather | solution.py:58
  403.8 8.4 %slice.9 = bf16[64,32,2048]{2,1,0:T(8,128)(2,1)} slice(bf16[64,40,2048]{2,1,0:T(8,128)(2,1)} %bitcast.39), slice={[0:64], [8:40], [0:2048]} | slice | bytes 16777216 | tf_op jit(solution)/shard_map/slice | solution.py:63
  412.1 6.3 %multiply_reduce_fusion.4 = (f32[42]{0:T(128)S(1)}, f32[2048,42]{0,1:T(8,128)S(1)}) fusion(f32[2048,42]{0,1:T(8,128)S(1)} %copy.31, bf16[2048,2048]{1,0:T(8,128)(2,1)} %bitcast.33, bf16[2048,42]{0,1:T(8,128)(2,1)S(1)} %convert_element_type.34), kind=kOutput, calls=%fused_computation.20 | convolution fusion | flops 352493536 | bytes 9248936 | tf_op jit(solution)/shard_map/dot_general | solution.py:20
  418.7 2.8 fusion.2
  421.5 2.4 fusion.28
  424.8 9.1 %all-to-all-start.1 = ((bf16[64,2,168]{2,1,0:T(2,128)(2,1)}), bf16[64,2,168]{2,1,0:T(2,128)(2,1)S(1)}, u32[]{:S(2)}, u32[]{:S(2)}) async-start(bf16[64,2,168]{2,1,0:T(2,128)(2,1)} %reshape.79), calls=%async_computation.1 | async-start | bytes 131072 | tf_op jit(solution)/shard_map/all_to_all | solution.py:80
  433.9 2.1 fusion
  436.0 6.1 %multiply_reduce_fusion.1 = (f32[42]{0:T(128)S(1)}, f32[42]{0:T(128)S(1)}, f32[2048,42]{0,1:T(8,128)S(1)}) fusion(f32[2048,42]{0,1:T(8,128)S(1)} %fusion, bf16[2048,2048]{1,0:T(8,128)(2,1)} %bitcast.34), kind=kOutput, calls=%fused_computation.14 | convolution fusion | flops 352751552 | bytes 9077072 | tf_op jit(solution)/shard_map/dot_general | solution.py:20
  442.4 6.2 %fusion.3 = f32[42]{0:T(128)S(1)} fusion(bf16[2048,2048]{1,0:T(8,128)(2,1)} %bitcast.35, f32[2048,42]{0,1:T(8,128)S(1)} %fusion, f32[2048,42]{0,1:T(8,128)S(1)} %get-tuple-element.8, f32[42]{0:T(128)S(1)} %div.54, f32[42]{0:T(128)S(1)} %div.53), kind=kOutput, calls=%fused_computation.6 | convolution fusion | flops 353267680 | bytes 9077240 | tf_op jit(solution)/shard_map/dot_general | solution.py:20
  449.1 2.1 reshape.81
  451.3 14.3 %all-to-all-start.2 = ((f32[64,1,1344]{2,1,0:T(1,128)}), f32[64,1,1344]{2,1,0:T(1,128)S(1)}, u32[]{:S(2)}, u32[]{:S(2)}) async-start(f32[64,1,1344]{2,1,0:T(1,128)} %reshape.81), calls=%async_computation.2 | async-start | bytes 720896 | tf_op jit(solution)/shard_map/all_to_all | solution.py:83
  466.6 18.1 %all-to-all-done.2 = f32[64,1,1344]{2,1,0:T(1,128)S(1)} async-done(((f32[64,1,1344]{2,1,0:T(1,128)}), f32[64,1,1344]{2,1,0:T(1,128)S(1)}, u32[]{:S(2)}, u32[]{:S(2)}) %all-to-all-start.2) | async-done | bytes 344096 | tf_op jit(solution)/shard_map/all_to_all | solution.py:83
  484.7 1.5 reduce.2
  486.1 1.4 reshape.82
  (46 shorter events, 12.7 us)
Async XLA Ops:
  7.2 252.6 %copy-start.1 = (s32[8]{0:T(128)S(1)}, s32[8]{0:T(128)}, u32[]{:S(2)}) copy-start(s32[8]{0:T(128)} %param.9) | copy-start | bytes 100
  7.2 147.6 %all-gather.3.cloned.1.call-start = ((), (), s32[]{:S(2)}) async-start(), calls=%async_computation.3 | async-start | bytes 4259840 | tf_op jit(solution)/shard_map/all_gather | solution.py:44
  7.9 228.2 %all-reduce.4.cloned.1.call-start = ((), (), s32[]{:S(2)}) async-start(), calls=%async_computation.4 | async-start | bytes 655360 | tf_op jit(solution)/shard_map/psum | solution.py:50
  159.1 244.6 %all-gather.5.cloned.1.call-start = ((), (), s32[]{:S(2)}) async-start(), calls=%async_computation.5 | async-start | bytes 10649600 | tf_op jit(solution)/shard_map/all_gather | solution.py:58
  243.1 47.7 %all-to-all-start = ((f32[64,1,1344]{2,1,0:T(1,128)}), f32[64,1,1344]{2,1,0:T(1,128)S(1)}, u32[]{:S(2)}, u32[]{:S(2)}) async-start(f32[64,1,1344]{2,1,0:T(1,128)} %reshape.77), calls=%async_computation | async-start | bytes 720896 | tf_op jit(solution)/shard_map/all_to_all | solution.py:64
  412.1 6.5 %copy-start = (bf16[64,32,2048]{2,1,0:T(8,128)(2,1)S(1)}, bf16[64,32,2048]{2,1,0:T(8,128)(2,1)}, u32[]{:S(2)}) copy-start(bf16[64,32,2048]{2,1,0:T(8,128)(2,1)} %slice.9) | copy-start | bytes 25165828
  424.8 26.5 %all-to-all-start.1 = ((bf16[64,2,168]{2,1,0:T(2,128)(2,1)}), bf16[64,2,168]{2,1,0:T(2,128)(2,1)S(1)}, u32[]{:S(2)}, u32[]{:S(2)}) async-start(bf16[64,2,168]{2,1,0:T(2,128)(2,1)} %reshape.79), calls=%async_computation.1 | async-start | bytes 131072 | tf_op jit(solution)/shard_map/all_to_all | solution.py:80
  451.3 33.4 %all-to-all-start.2 = ((f32[64,1,1344]{2,1,0:T(1,128)}), f32[64,1,1344]{2,1,0:T(1,128)S(1)}, u32[]{:S(2)}, u32[]{:S(2)}) async-start(f32[64,1,1344]{2,1,0:T(1,128)} %reshape.81), calls=%async_computation.2 | async-start | bytes 720896 | tf_op jit(solution)/shard_map/all_to_all | solution.py:83
Sparse Core Ops, SparseCore 0:
  11.0 143.7 all-gather.2
  159.3 76.8 all-reduce.3
  240.1 163.6 all-gather.4
where the time goes:
time: 504 us; the launch traced here: 496 us
  waiting for transfers between devices  348 us (69%)
  starting transfers between devices  38.3 us (8%)
  blocking collectives  30.8 us (6%)
  matrix products  30.1 us (6%)
  local copies, waits for them, and re-layouts  27.9 us (6%)
  between operations  14.7 us (3%)
  other arithmetic  6.6 us (1%)
    all_gather x1, waiting for transfers between devices, local(): lax.all_gather(support_feats, 'sup', axis=0, tiled=True)  147 us
    all_gather x1, waiting for transfers between devices, local(): lax.all_gather((scaled + jnp.where(on_diag, RIDGE, 0.0)).astype(jnp.bfloa...  107 us
    psum x1, waiting for transfers between devices, local(): summed = lax.psum(partial_gram, 'cls')  75.4 us
    unnamed x1, blocking collectives  30.8 us
    dot_general x4, matrix products, conjugate(): jnp.dot(kernel, direction.astype(jnp.bfloat16), preferred_element_type=jn...  21.3 us
    all_to_all x1, waiting for transfers between devices, local(): lax.all_to_all(hyper_cols, 'sup', split_axis=0, concat_axis=1, tiled=True)  18.1 us
    all_to_all x1, starting transfers between devices, local(): lax.all_to_all(soft_labels, 'sup', split_axis=1, concat_axis=0, tiled=True)  14.7 us
    all_to_all x1, starting transfers between devices, local(): lax.all_to_all(hyper_cols, 'sup', split_axis=0, concat_axis=1, tiled=True)  14.3 us
  transfers between devices with their start and end apart: 6, of which 4 were waited for; matrix products, arithmetic and copies ran while one was open for 6% of the time, Pallas kernels for 0%

commit v1 on v0

v1 whole, which is shorter than its diff:
```python
import functools

import jax
import jax.numpy as jnp
from jax import lax
from jax.experimental import pallas as pl
from jax.experimental.pallas import tpu as pltpu
from jax.sharding import PartitionSpec as P

MESH = pl.DeviceIdType.MESH
F = 8192
RIDGE = 0.05
LABEL_SCALE = 16.0

NZ, NY, NX = 16, 4, 4
NSUP = NZ * NY
ROWS = 32
TROWS = 8
LANES = 128
BLOCKS = 21
PIECE = LANES + NY * TROWS
HALF = PIECE // 2
SENT = ROWS + 1
CELL = 40
F32 = jnp.float32
BF16 = jnp.bfloat16


def place():
    sup = lax.axis_index("sup")
    cls = lax.axis_index("cls")
    return sup // NY, sup % NY, cls // 2, cls % 2


def device(z, y, x, core):
    return {"sup": z * NY + y, "cls": x * 2 + core}


def signal(sem, dev):
    pl.semaphore_signal(sem, inc=1, device_id=dev, device_id_type=MESH)


def send(src, dst, send_sem, recv_sem, dev):
    pltpu.make_async_remote_copy(
        src_ref=src, dst_ref=dst, send_sem=send_sem, recv_sem=recv_sem, device_id=dev, device_id_type=MESH
    ).start()


def arrive(ref, sem):
    pltpu.make_async_copy(ref, ref, sem).wait()


def gram_kernel(feats, targets, scales, piece, jbuf, ibuf, tbuf, part, rbuf, zs, zr, ys, yr, ts, tr, xs, xr):
    z, y, x, core = place()
    up, down = (z + 1) % NZ, (z + NZ - 1) % NZ

    jbuf[z] = feats[...]
    ibuf[y] = feats[...]
    tfeats = targets[...].astype(F32)
    tbuf[y] = jnp.concatenate([tfeats, jnp.zeros_like(tfeats)], axis=0).astype(BF16)

    barrier = pltpu.get_barrier_semaphore()
    signal(barrier, device(up, y, x, core))
    signal(barrier, device(down, y, x, core))
    for k in range(1, NY):
        signal(barrier, device(z, (y + k) % NY, x, core))

    @pl.when(core == 0)
    def _():
        signal(barrier, device(z, y, x, 1))
        for k in range(1, NX):
            signal(barrier, device(z, y, (x + k) % NX, 0))
            signal(barrier, device(z, y, (x + k) % NX, 1))

    pl.semaphore_wait(barrier, 2 + NY - 1 + NX - 1 + core)

    def round_z(k):
        right, left = jbuf.at[(z + NZ - k) % NZ], jbuf.at[(z + k) % NZ]
        if k == NZ // 2 - 1:
            right, left = right.at[pl.ds(0, ROWS // 2)], left.at[pl.ds(ROWS // 2, ROWS // 2)]
        send(right, right, zs.at[0, k], zr.at[0, k], device(up, y, x, core))
        send(left, left, zs.at[1, k], zr.at[1, k], device(down, y, x, core))

    def wait_z(k):
        ref = jbuf.at[z]
        if k == NZ // 2 - 1:
            ref = ref.at[pl.ds(0, ROWS // 2)]
        arrive(ref, zr.at[0, k])
        arrive(ref, zr.at[1, k])

    round_z(0)
    for k in range(1, NY):
        dev = device(z, (y + k) % NY, x, core)
        send(ibuf.at[y], ibuf.at[y], ys.at[k - 1], yr.at[k - 1], dev)
        send(tbuf.at[y], tbuf.at[y], ts.at[k - 1], tr.at[k - 1], dev)
    for k in range(1, NZ // 2):
        wait_z(k - 1)
        round_z(k)
    for k in range(1, NY):
        arrive(ibuf.at[y], yr.at[k - 1])
        arrive(tbuf.at[y], tr.at[k - 1])
    wait_z(NZ // 2 - 1)

    cols = jbuf[...].reshape(NZ * ROWS, -1)
    over = (((1,), (1,)), ((), ()))
    gram = lax.dot_general(cols, ibuf[...].reshape(NY * ROWS, -1), over, preferred_element_type=F32)
    cross = lax.dot_general(tbuf[...].reshape(NY * 16, -1), cols, over, preferred_element_type=F32)
    cross = cross.reshape(NY, 16, NZ * ROWS)[:, :TROWS].reshape(NY * TROWS, NZ * ROWS)
    for k in range(NX):
        part[k, 0:LANES] = gram[k * LANES : (k + 1) * LANES]
        part[k, LANES:PIECE] = cross[:, k * LANES : (k + 1) * LANES]

    own = x * 2 + core
    for k in range(1, NX):
        to = (x + k) % NX
        send(part.at[to], rbuf.at[own], xs.at[k], xr, device(z, y, to, 0))

    @pl.when(core == 1)
    def _():
        send(part.at[x], rbuf.at[own], xs.at[0], xr, device(z, y, x, 0))
        arrive(part.at[x], xs.at[0])
        piece[...] = jnp.zeros_like(piece)

    @pl.when(core == 0)
    def _():
        rbuf[own] = part[x]
        arrive(rbuf.at[pl.ds(0, 2 * NX - 1)], xr)
        total = rbuf[0]
        for k in range(1, 2 * NX):
            total = total + rbuf[k]
        col_scale = scales[pl.ds(z, 1), :]
        lane = lax.broadcasted_iota(jnp.int32, (ROWS, LANES), 1)
        row = lax.broadcasted_iota(jnp.int32, (ROWS, LANES), 0)
        row_scales = []
        for a in range(4):
            zz = x * 4 + a
            picked = jnp.where(lane == y * ROWS + row, scales[pl.ds(zz, 1), :], 0.0)
            row_scale = jnp.sum(picked, axis=1, keepdims=True)
            row_scales.append(row_scale)
            diag = zz * LANES + y * ROWS + row == z * LANES + lane
            block = total[a * ROWS : (a + 1) * ROWS] * (row_scale * col_scale) / F
            piece[a * ROWS : (a + 1) * ROWS] = (block + jnp.where(diag, RIDGE, 0.0)).astype(BF16)
        row_scale = jnp.concatenate(row_scales, axis=0)
        same = lax.broadcasted_iota(jnp.int32, (LANES, LANES), 0) == lax.broadcasted_iota(jnp.int32, (LANES, LANES), 1)
        cross_scale = jnp.sum(jnp.where(same, row_scale, 0.0), axis=0, keepdims=True)
        piece[LANES:PIECE] = (total[LANES:PIECE] * cross_scale / F).astype(BF16)

    for k in range(1, NX):
        arrive(part.at[x], xs.at[k])
    for k in range(1, NY):
        arrive(ibuf.at[y], ys.at[k - 1])
        arrive(tbuf.at[y], ts.at[k - 1])
    for k in range(NZ // 2):
        ref = jbuf.at[z]
        if k == NZ // 2 - 1:
            ref = ref.at[pl.ds(0, ROWS // 2)]
        arrive(ref, zs.at[0, k])
        arrive(ref, zs.at[1, k])


def worker_sup(w):
    return (w * 32) // 21


def solve_kernel(
    piece, labels, classes, pred_out, hyper_out,
    kbuf, stage, bbuf, hbuf, pbuf, pn, bvec, vec, dvec, low, pred, hst,
    ls, lr, fs, fr, zs, zr, ds, dr, ws, wr, ps, pr, hs, hr,
):
    z, y, x, core = place()
    sup = z * NY + y
    up, down = (z + 1) % NZ, (z + NZ - 1) % NZ
    w = (sup * 21 + 31) // 32
    is_worker = (core == 0) & (worker_sup(w) == sup) & (w < 2 * BLOCKS)
    served = w // BLOCKS
    block = w % BLOCKS
    own_worker = is_worker & (served == 0)

    def to_worker(j):
        return worker_sup(core * BLOCKS + j)

    barrier = pltpu.get_barrier_semaphore()

    @pl.when(core == 0)
    def _():
        signal(barrier, device(up, y, x, 0))
        signal(barrier, device(down, y, x, 0))
        for k in range(1, NY):
            signal(barrier, device(z, (y + k) % NY, x, 0))
            signal(barrier, device(z, y, (x + k) % NX, 0))

    def greet_worker(j, c):
        to = to_worker(j)

        @pl.when((core == 1) | (to != sup))
        def _():
            signal(barrier, {"sup": to, "cls": x * 2})

        return c

    lax.fori_loop(0, BLOCKS, greet_worker, 0)

    @pl.when(is_worker)
    def _():
        def greet(s, c):
            @pl.when((served == 1) | (s != sup))
            def _():
                signal(barrier, {"sup": s, "cls": x * 2 + served})

            return c

        lax.fori_loop(0, NSUP, greet, 0)

    for j in range(BLOCKS):
        stage[j, 0:ROWS] = labels[:, j * LANES : (j + 1) * LANES]
        stage[j, ROWS:CELL] = classes[...]

    @pl.when(core == 0)
    def _():
        kbuf[z, y, x] = piece[...]

    peers = BLOCKS + jnp.where(core == 0, 2 + NY - 1 + NX - 1, 0)
    peers = peers + jnp.where(is_worker, NSUP, 0) - jnp.where(own_worker, 2, 0)
    pl.semaphore_wait(barrier, peers)

    def chunk(path, zz, pos, h=None):
        inner = pl.ds(0, 4) if h is None else pl.ds(2 * h, 2)
        if path == 0:
            return kbuf.at[zz, pos, inner, pl.ds(0, HALF)]
        return kbuf.at[zz, inner, pos, pl.ds(HALF, HALF)]

    pos = (y, x)

    def last_dev(path, k):
        if path == 0:
            return device(z, (y + k) % NY, x, 0)
        return device(z, y, (x + k) % NX, 0)

    @pl.when(core == 0)
    def _():
        for k in range(1, 4):
            own = kbuf.at[z, y, x, pl.ds(0, HALF)]
            send(own, own, fs.at[0, k - 1], fr.at[0, k - 1], device(z, y, (x + k) % NX, 0))
            own = kbuf.at[z, y, x, pl.ds(HALF, HALF)]
            send(own, own, fs.at[1, k - 1], fr.at[1, k - 1], device(z, (y + k) % NY, x, 0))

    def send_label(j, c):
        to = to_worker(j)

        @pl.when((core == 1) | (to != sup))
        def _():
            send(stage.at[j, pl.ds(0, SENT)], bbuf.at[sup, pl.ds(0, SENT)], ls, lr, {"sup": to, "cls": x * 2})

        return c

    lax.fori_loop(0, BLOCKS, send_label, 0)

    @pl.when(own_worker)
    def _():
        bbuf[sup] = stage[block]

    @pl.when(core == 0)
    def _():
        def forward(path, zz):
            me = pos[path]
            arrive(chunk(path, zz, me), dr.at[path, 0, zz])
            ref = chunk(path, zz, (me + 3) % 4, 0)
            send(ref, ref, ws.at[path, 0], wr.at[path, 0, zz], last_dev(path, 1))
            arrive(chunk(path, zz, me), dr.at[path, 1, zz])
            ref = chunk(path, zz, (me + 1) % 4, 1)
            send(ref, ref, ws.at[path, 1], wr.at[path, 1, zz], last_dev(path, 3))

        def having(k):
            if k == 0:
                return [z]
            if k == NZ // 2:
                return [(z + k) % NZ]
            return [(z + NZ - k) % NZ, (z + k) % NZ]

        last = NZ // 2
        for k in range(last + 2):
            for path in range(2):
                me = pos[path]
                if k <= last:
                    if k == 0:
                        for i in range(3):
                            arrive(kbuf.at[z, y, x, pl.ds(0, HALF)], fr.at[path, i])
                    else:
                        h = None if k < last else 0
                        arrive(chunk(path, z, me, h), zr.at[path, 0, k - 1])
                        arrive(chunk(path, z, me, h), zr.at[path, 1, k - 1])
                    if k < last:
                        right = chunk(path, (z + NZ - k) % NZ, me, None if k < last - 1 else 0)
                        left = chunk(path, (z + k) % NZ, me, None if k < last - 1 else 1)
                        send(right, right, zs.at[path, 0], zr.at[path, 0, k], device(up, y, x, 0))
                        send(left, left, zs.at[path, 1], zr.at[path, 1, k], device(down, y, x, 0))
                    for zz in having(k):
                        ref = chunk(path, zz, me)
                        send(ref, ref, ds.at[path, 0], dr.at[path, 0, zz], last_dev(path, 1))
                        send(ref, ref, ds.at[path, 1], dr.at[path, 1, zz], last_dev(path, 3))
                if k > 0:
                    for zz in having(k - 1):
                        forward(path, zz)
        for path in range(2):
            for zz in range(NZ):
                arrive(chunk(path, zz, pos[path], 0), wr.at[path, 0, zz])
                arrive(chunk(path, zz, pos[path], 0), wr.at[path, 1, zz])

    @pl.when(is_worker)
    def _():
        @pl.when(served == 0)
        def _():
            arrive(bbuf.at[pl.ds(0, NSUP - 1), pl.ds(0, SENT)], lr)

        @pl.when(served == 1)
        def _():
            arrive(bbuf.at[:, pl.ds(0, SENT)], lr)

        def rows_of(r):
            return pl.ds(pl.multiple_of(r * 256, 256), 256)

        def product(r):
            lhs = jnp.concatenate(
                [kbuf[zz, r // 2, pl.ds((r % 2) * 2, 2), 0:LANES, :].reshape(256, LANES) for zz in range(NZ)], axis=1
            )
            return jnp.dot(lhs, pn[...].reshape(NZ * LANES, LANES), preferred_element_type=F32)

        def fold(v):
            return jnp.sum(v.reshape(32, 8, LANES), axis=0)

        def total(v):
            return jnp.sum(v, axis=0, keepdims=True)

        def to_natural(r, v):
            pn[pl.ds((r % 2) * 8, 8), r // 2] = v.reshape(8, ROWS, LANES).astype(BF16)

        zero = jnp.zeros((8, LANES), F32)

        def solve(emit):
            def first(r, c):
                image = product(r)
                b = bvec[rows_of(r), :]
                vec[rows_of(r), :] = image
                return c[0] + fold(b * b), c[1] + fold(b * image)

            norm, curve = lax.fori_loop(0, 8, first, (zero, zero))
            norm, curve = total(norm), total(curve)
            step0 = norm / curve

            def resid(r, c):
                v = bvec[rows_of(r), :] - step0 * vec[rows_of(r), :]
                vec[rows_of(r), :] = v
                return c + fold(v * v)

            norm1 = total(lax.fori_loop(0, 8, resid, zero))
            beta = norm1 / norm

            def turn(r, c):
                v = vec[rows_of(r), :] + beta * bvec[rows_of(r), :]
                dvec[rows_of(r), :] = v
                to_natural(r, v)
                return c

            lax.fori_loop(0, 8, turn, 0)

            def second(r, c):
                return c + fold(dvec[rows_of(r), :] * product(r))

            step1 = norm1 / total(lax.fori_loop(0, 8, second, zero))

            def finish(r, c):
                emit(r, step0 * bvec[rows_of(r), :] + step1 * dvec[rows_of(r), :])
                return c

            lax.fori_loop(0, 8, finish, 0)

        def load(r, c):
            b = bbuf.reshape(NZ, NY, CELL, LANES)[pl.ds((r % 2) * 8, 8), r // 2, 0:ROWS, :]
            bvec[rows_of(r), :] = b.reshape(256, LANES)
            pn[pl.ds((r % 2) * 8, 8), r // 2] = b.astype(BF16)
            return c

        lax.fori_loop(0, 8, load, 0)

        def keep_low(r, v):
            low[rows_of(r), :] = v.astype(BF16)

        solve(keep_low)

        crosses = [kbuf[:, q // NX, q % NX, LANES:PIECE, :].reshape(512, LANES) for q in range(16)]
        predicted = jnp.dot(jnp.concatenate(crosses, axis=1), low[...], preferred_element_type=F32)
        pred[...] = predicted.reshape(NSUP, TROWS, LANES)

        at = pl.ds(pl.multiple_of(block * LANES, LANES), LANES)

        def send_pred(s, c):
            @pl.when((served == 1) | (s != sup))
            def _():
                send(pred.at[s], pbuf.at[:, at], ps, pr, {"sup": s, "cls": x * 2 + served})

            return c

        lax.fori_loop(0, NSUP, send_pred, 0)

        @pl.when(served == 0)
        def _():
            pbuf[:, at] = pred[sup]

        lane = lax.broadcasted_iota(jnp.int32, (NSUP, TROWS, LANES), 2)
        row = lax.broadcasted_iota(jnp.int32, (NSUP, TROWS, LANES), 1)
        target = jnp.sum(jnp.where(lane == row, bbuf[:, ROWS : ROWS + 1, :], 0.0), axis=2, keepdims=True)
        first_class = ((x * 2 + served) * BLOCKS + block) * LANES
        onehot = jnp.where(target == (first_class + lane).astype(F32), LABEL_SCALE, 0.0)
        misfit = (predicted - onehot.reshape(512, LANES)).astype(BF16)
        for q in range(16):
            cross = kbuf[:, q // NX, q % NX, LANES:PIECE, :].reshape(512, LANES)
            rhs = lax.dot_general(cross, misfit, (((0,), (0,)), ((), ())), preferred_element_type=F32)
            bvec[q * LANES : (q + 1) * LANES, :] = rhs
            for a in range(4):
                pn[(q % NX) * 4 + a, q // NX] = rhs[a * ROWS : (a + 1) * ROWS].astype(BF16)

        def keep_hyper(r, v):
            hst[pl.ds((r % 2) * 8, 8), r // 2] = v.reshape(8, ROWS, LANES).astype(BF16)

        solve(keep_hyper)

        def send_hyper(s, c):
            @pl.when((served == 1) | (s != sup))
            def _():
                send(hst.at[s // NY, s % NY], hbuf.at[:, at], hs, hr, {"sup": s, "cls": x * 2 + served})

            return c

        lax.fori_loop(0, NSUP, send_hyper, 0)

        @pl.when(served == 0)
        def _():
            hbuf[:, at] = hst[z, y]

    def collect(buf, sem):
        @pl.when(own_worker)
        def _():
            arrive(buf.at[:, pl.ds(0, (BLOCKS - 1) * LANES)], sem)

        @pl.when(jnp.logical_not(own_worker))
        def _():
            arrive(buf, sem)

    collect(pbuf, pr)
    pred_out[...] = pbuf[...].astype(BF16)
    collect(hbuf, hr)
    hyper_out[...] = hbuf[...].astype(F32)

    @pl.when(own_worker)
    def _():
        arrive(stage.at[pl.ds(0, BLOCKS - 1), pl.ds(0, SENT)], ls)

    @pl.when(jnp.logical_not(own_worker))
    def _():
        arrive(stage.at[:, pl.ds(0, SENT)], ls)

    @pl.when(core == 0)
    def _():
        for path in range(2):
            for i in range(3):
                arrive(kbuf.at[z, y, x, pl.ds(0, HALF)], fs.at[path, i])
            for d in range(2):
                arrive(kbuf.at[pl.ds(0, NZ - 1), 0, pl.ds(0, 2), pl.ds(0, HALF)], zs.at[path, d])
                arrive(kbuf.at[:, 0, :, pl.ds(0, HALF)], ds.at[path, d])
                arrive(kbuf.at[:, 0, pl.ds(0, 2), pl.ds(0, HALF)], ws.at[path, d])

    @pl.when(is_worker & (served == 0))
    def _():
        arrive(pred.at[pl.ds(0, NSUP - 1)], ps)
        arrive(low.at[pl.ds(0, (NSUP - 1) * ROWS)], hs)

    @pl.when(is_worker & (served == 1))
    def _():
        arrive(pred, ps)
        arrive(hst, hs)


def vmem():
    return pl.BlockSpec(memory_space=pltpu.VMEM)


def local(support_feats, target_feats, scales, soft_labels, target_labels):
    width = support_feats.shape[1]
    dma = pltpu.SemaphoreType.DMA
    piece = pl.pallas_call(
        gram_kernel,
        out_shape=jax.ShapeDtypeStruct((PIECE, LANES), BF16),
        in_specs=[vmem()] * 3,
        out_specs=vmem(),
        scratch_shapes=[
            pltpu.VMEM((NZ, ROWS, width), BF16),
            pltpu.VMEM((NY, ROWS, width), BF16),
            pltpu.VMEM((NY, 16, width), BF16),
            pltpu.VMEM((NX, PIECE, LANES), F32),
            pltpu.VMEM((2 * NX, PIECE, LANES), F32),
            dma((2, NZ // 2)), dma((2, NZ // 2)),
            dma((NY - 1,)), dma((NY - 1,)), dma((NY - 1,)), dma((NY - 1,)),
            dma((NX,)), dma,
        ],
        compiler_params=pltpu.CompilerParams(collective_id=0, has_side_effects=True, vmem_limit_bytes=24 * 2**20),
        name="gram",
    )(support_feats, target_feats, scales.astype(F32).reshape(NZ, LANES))

    classes = jnp.zeros((CELL - ROWS, LANES), F32).at[:, 0:TROWS].set(target_labels.astype(F32)[None, :])
    return pl.pallas_call(
        solve_kernel,
        out_shape=(
            jax.ShapeDtypeStruct((TROWS, BLOCKS * LANES), BF16),
            jax.ShapeDtypeStruct((ROWS, BLOCKS * LANES), F32),
        ),
        in_specs=[vmem()] * 3,
        out_specs=(vmem(), vmem()),
        scratch_shapes=[
            pltpu.VMEM((NZ, NY, NX, PIECE, LANES), BF16),
            pltpu.VMEM((BLOCKS, CELL, LANES), F32),
            pltpu.VMEM((NSUP, CELL, LANES), F32),
            pltpu.VMEM((ROWS, BLOCKS * LANES), BF16),
            pltpu.VMEM((TROWS, BLOCKS * LANES), F32),
            pltpu.VMEM((NZ, NY, ROWS, LANES), BF16),
            pltpu.VMEM((2048, LANES), F32),
            pltpu.VMEM((2048, LANES), F32),
            pltpu.VMEM((2048, LANES), F32),
            pltpu.VMEM((2048, LANES), BF16),
            pltpu.VMEM((NSUP, TROWS, LANES), F32),
            pltpu.VMEM((NZ, NY, ROWS, LANES), BF16),
            dma, dma,
            dma((2, 3)), dma((2, 3)),
            dma((2, 2)), dma((2, 2, NZ // 2)),
            dma((2, 2)), dma((2, 2, NZ)),
            dma((2, 2)), dma((2, 2, NZ)),
            dma, dma, dma, dma,
        ],
        compiler_params=pltpu.CompilerParams(collective_id=1, has_side_effects=True, vmem_limit_bytes=44 * 2**20),
        name="solve",
    )(piece, soft_labels, classes)


def solution(mesh):
    in_specs = (P("sup", "cls"), P("sup", "cls"), P(), P("sup", "cls"), P("sup"))
    out_specs = (P("sup", "cls"), P("sup", "cls"))
    return jax.shard_map(local, mesh=mesh, in_specs=in_specs, out_specs=out_specs, check_vma=False)
```

time: 504 us -> 151 us (0.30); the launches traced: 496 us -> 148 us
  waiting for transfers between devices: 348 us -> 0 us
  Pallas kernels: 0 us -> 142 us
  starting transfers between devices: 38.3 us -> 0 us
  blocking collectives: 30.8 us -> 0 us
  matrix products: 30.1 us -> 0 us
  local copies, waits for them, and re-layouts: 27.9 us -> 3.18 us
  between operations: 14.7 us -> 0.7 us
    all_gather x2 -> x0, waiting for transfers between devices: 253 us -> none  [the longest x1 147 us: local(): lax.all_gather(support_feats, 'sup', axis=0, tiled=True)]
    pallas_call x0 -> x2, Pallas kernels: none -> 142 us  [the longest x1 102 us: local(): pl.pallas_call(solve_kernel, out_shape=(jax.ShapeDtypeStruct((TROWS, BLOC...]
    psum x1 -> x0, waiting for transfers between devices: 75.4 us -> none  [local(): summed = lax.psum(partial_gram, 'cls')]
    all_to_all x3 -> x0, starting transfers between devices: 38.1 us -> none  [the longest x1 14.7 us: local(): lax.all_to_all(soft_labels, 'sup', split_axis=1, concat_axis=0, tiled=True)]
    unnamed x1 -> x0, blocking collectives: 30.8 us -> none
    dot_general x7 -> x0, matrix products: 30.1 us -> none  [the longest x4 21.3 us: conjugate(): jnp.dot(kernel, direction.astype(jnp.bfloat16), preferred_element_type=jn...]
    all_to_all x3 -> x0, waiting for transfers between devices: 18.1 us -> none  [the longest x1 18.1 us: local(): lax.all_to_all(hyper_cols, 'sup', split_axis=0, concat_axis=1, tiled=True)]
    slice x1 -> x0, local copies, waits for them, and re-layouts: 8.39 us -> none  [local(): blocks[:, own_targets:].reshape(support_total, support_total)]
  transfers between devices with their start and end apart: 6 -> 0, of which waited for: 4 -> 0; matrix products, arithmetic and copies ran while one was open for 6% -> 0% of each run, Pallas kernels for 0% -> 0%
where the time goes in v1:
time: 151 us; the launch traced here: 148 us
  Pallas kernels  142 us (94%)
  local copies, waits for them, and re-layouts  3.18 us (2%)
  other arithmetic  1.98 us (1%)
    pallas_call x1, Pallas kernels, local(): pl.pallas_call(solve_kernel, out_shape=(jax.ShapeDtypeStruct((TROWS, BLOC...  102 us
    pallas_call x1, Pallas kernels, local(): pl.pallas_call(gram_kernel, out_shape=jax.ShapeDtypeStruct((PIECE, LANES)...  40.7 us
    unnamed x10, local copies, waits for them, and re-layouts  3.17 us

profile of v1, /device:TPU:1, one launch (start us, length us, event | category | flops | bytes accessed | tf_op | source)
XLA Modules:
  0.0 148.3 jit_solution(8939511594892725511)
XLA Ops:
  0.6 0.0 copy-start.3
  0.6 0.0 copy-start.2
  0.6 0.6 compare_reduce_fusion
  1.3 0.0 copy-done.3
  1.3 0.6 broadcast_select_fusion
  2.0 0.7 bitcast_convert_fusion.scales
  2.7 0.0 copy-done.2
  2.7 0.0 copy-start.1
  2.7 0.8 copy-done.1
  3.5 40.7 %gram.1.piece = bf16[160,128]{1,0:T(8,128)(2,1)S(1)} custom-call(bf16[32,1024]{1,0:T(8,128)(2,1)S(1)} %copy-done.1, bf16[8,1024]{1,0:T(8,128)(2,1)S(1)} %copy-done.2, f32[16,128]{1,0:T(8,128)S(1)} %bitcast_convert_fusion.scales), custom_call_target="tpu_custom_call" | custom-call | tf_op jit(solution)/shard_map/gram/pallas_call | solution.py:490
  44.2 0.0 copy-start
  44.2 1.0 copy-done
  45.2 101.8 %solve.1 = (bf16[8,2688]{1,0:T(8,128)(2,1)S(1)}, f32[32,2688]{1,0:T(8,128)S(1)}) custom-call(bf16[160,128]{1,0:T(8,128)(2,1)S(1)} %gram.1.piece, f32[32,2688]{1,0:T(8,128)S(1)} %copy-done, f32[8,128]{1,0:T(8,128)S(1)} %scatter.8.classes), custom_call_target="tpu_custom_call" | custom-call | tf_op jit(solution)/shard_map/solve/pallas_call | solution.py:510
  146.9 0.6 copy.9
  147.6 0.7 copy.10
  (2 shorter events, 0.0 us)
Async XLA Ops:
  0.6 0.7 copy-start.3
  0.6 2.0 %copy-start.2 = (bf16[8,1024]{1,0:T(8,128)(2,1)S(1)}, bf16[8,1024]{1,0:T(8,128)(2,1)}, u32[]{:S(2)}) copy-start(bf16[8,1024]{1,0:T(8,128)(2,1)} %targets.1) | copy-start | bytes 49156
  2.7 0.8 copy-start.1
  44.2 1.0 copy-start

commit v2 on v0

v2 whole, which is shorter than its diff:
```python
import functools

import jax
import jax.numpy as jnp
from jax import lax
from jax.experimental import pallas as pl
from jax.experimental.pallas import tpu as pltpu
from jax.sharding import PartitionSpec as P

MESH = pl.DeviceIdType.MESH
F = 8192
RIDGE = 0.05
LABEL_SCALE = 16.0

NZ, NY, NX = 16, 4, 4
NSUP = NZ * NY
ROWS = 32
TROWS = 8
LANES = 128
BLOCKS = 21
PIECE = LANES + NY * TROWS
HALF = PIECE // 2
KPART, CPART = LANES // 2, NY * TROWS // 2
WINDOW = (0, 1, -1, 2)
F32 = jnp.float32
BF16 = jnp.bfloat16


def place():
    sup = lax.axis_index("sup")
    cls = lax.axis_index("cls")
    return sup // NY, sup % NY, cls // 2, cls % 2


def device(z, y, x, core):
    return {"sup": z * NY + y, "cls": x * 2 + core}


def signal(sem, dev):
    pl.semaphore_signal(sem, inc=1, device_id=dev, device_id_type=MESH)


def send(src, dst, send_sem, recv_sem, dev):
    pltpu.make_async_remote_copy(
        src_ref=src, dst_ref=dst, send_sem=send_sem, recv_sem=recv_sem, device_id=dev, device_id_type=MESH
    ).start()


def arrive(ref, sem):
    pltpu.make_async_copy(ref, ref, sem).wait()


def worker_sup(w, x):
    v = (w * 8) // 7
    return (v // 3) * NY + (v % 3 + 8 - x) % NY


def kernel(
    feats, targets, scales, labels, classes, pbuf, hbuf,
    ibuf, tbuf, jbuf, part, rbuf, kbuf, cstage, cbuf, bbuf, pn, bvec, vec, low, pred, hst,
    wide, iws, iwr, tws, twr, iys, iyr, tys, tyr, js, jr, xs, xr,
    ls, lr, cs, cr, s1, r1, s2, r2, s4, r4, s5, r5, s6, r6, s7, ps, pr, hs, hr,
):
    z, y, x, core = place()
    sup = z * NY + y
    zq, zr = z // 4, z % 4
    kind = (y + x) % 4
    v = z * 3 + kind
    w = (v * 7 + 7) // 8
    is_worker = (core == 0) & (kind < 3) & ((w * 8) // 7 == v) & (w < 2 * BLOCKS)
    served = w // BLOCKS
    block = w % BLOCKS
    own_worker = is_worker & (served == 0)
    others = jnp.logical_not(own_worker)

    def zshift(d):
        return (z + NZ + d) % NZ

    barrier = pltpu.get_barrier_semaphore()
    for t in range(1, 4):
        signal(barrier, device(zshift(WINDOW[t]), y, x, core))
        signal(barrier, device(zshift(4 * t), y, x, core))
        signal(barrier, device(z, (y + t) % NY, x, core))

    @pl.when(core == 0)
    def _():
        for t in range(1, 4):
            signal(barrier, device(z, y, (x + t) % NX, 0))
            signal(barrier, device(z, y, (x + t) % NX, 1))
            signal(barrier, device(zshift(4 * t), y, x, 1))
        signal(barrier, device(z, y, x, 1))

    own_window = pltpu.make_async_copy(feats, ibuf.at[0, y], s7)
    own_stride = pltpu.make_async_copy(feats, jbuf.at[zq], s1)
    own_window.start()
    own_stride.start()
    tf = targets[...].astype(F32)
    half = tf.shape[1] // 2
    tbuf[0, y] = jnp.concatenate([tf[:, :half], tf[:, half:]], axis=0).astype(BF16)
    lane8 = lax.broadcasted_iota(jnp.int32, (8, LANES), 1)
    row8 = jnp.zeros((8, LANES), jnp.int32)
    for i in range(TROWS):
        row8 = jnp.where(lane8 == i, classes[i], row8)
    cstage[...] = row8.astype(F32)
    wide[...] = scales[...].astype(F32)

    own_window.wait()
    own_stride.wait()
    pl.semaphore_wait(barrier, 3 * 4 + 4 * core)

    def spread(t, i):
        dev = device(z, (y + i) % NY, x, core)
        send(ibuf.at[t, y], ibuf.at[t, y], iys.at[t, i - 1], iyr.at[t, i - 1], dev)
        send(tbuf.at[t, y], tbuf.at[t, y], tys.at[t, i - 1], tyr.at[t, i - 1], dev)

    for t in range(1, 4):
        dev = device(zshift(-WINDOW[t]), y, x, core)
        send(ibuf.at[0, y], ibuf.at[t, y], iws.at[t - 1], iwr.at[t - 1], dev)
        send(tbuf.at[0, y], tbuf.at[t, y], tws.at[t - 1], twr.at[t - 1], dev)
        spread(0, t)
    for i in (2, 1, 3):
        send(jbuf.at[zq], jbuf.at[zq], js.at[i - 1], jr.at[i - 1], device(zshift(4 * i), y, x, core))
    for t in range(1, 4):
        arrive(ibuf.at[t, y], iwr.at[t - 1])
        arrive(tbuf.at[t, y], twr.at[t - 1])
        for i in range(1, 4):
            spread(t, i)
    for i in range(3):
        arrive(jbuf.at[zq], jr.at[i])
    for t in range(4):
        for i in range(3):
            arrive(ibuf.at[t, y], iyr.at[t, i])
            arrive(tbuf.at[t, y], tyr.at[t, i])

    over = (((1,), (1,)), ((), ()))
    own = x * 2 + core
    cols = jbuf[...].reshape(4 * ROWS, -1)
    for t in range(NX):
        part[t, 0:LANES] = lax.dot_general(
            cols, ibuf[t].reshape(NY * ROWS, -1), over, preferred_element_type=F32
        )
        low_t = tbuf[t].reshape(NY * 16, half)
        cross0 = lax.dot_general(low_t, cols[:, :half], over, preferred_element_type=F32)
        cross1 = lax.dot_general(low_t, cols[:, half:], over, preferred_element_type=F32)
        cross = cross0.reshape(NY, 16, LANES)[:, :TROWS] + cross1.reshape(NY, 16, LANES)[:, TROWS:]
        part[t, LANES:PIECE] = cross.reshape(NY * TROWS, LANES)

        @pl.when((core == 1) | (x != t))
        def _():
            send(part.at[t], rbuf.at[own], xs, xr, device(z, y, t, 0))

    def send_label(i, c):
        j = ((sup * 21) // 64 + i) % BLOCKS
        to = worker_sup(core * BLOCKS + j, x)

        @pl.when((core == 1) | (to != sup))
        def _():
            dev = {"sup": to, "cls": x * 2}
            send(labels.at[:, pl.ds(pl.multiple_of(j * LANES, LANES), LANES)], bbuf.at[sup], ls, lr, dev)
            send(cstage.at[pl.ds(0, 1)], cbuf.at[sup, pl.ds(0, 1)], cs, cr, dev)

        return c

    def send_labels():
        lax.fori_loop(0, BLOCKS, send_label, 0)

    pl.when(core == 1)(send_labels)

    @pl.when(own_worker)
    def _():
        own_labels = pltpu.make_async_copy(
            labels.at[:, pl.ds(pl.multiple_of(block * LANES, LANES), LANES)], bbuf.at[sup], s7
        )
        own_labels.start()
        own_labels.wait()
        cbuf[sup] = cstage[...]

    @pl.when(core == 0)
    def _():
        gather_pieces(
            z, y, x, zq, zr, kind, zshift, send_labels, wide, part, rbuf, kbuf, xr, own,
            s1, r1, s2, r2, s4, r4, s5, r5, s6, r6,
        )

    def arrive_rows(t):
        for path in range(2):
            for i in range(3):
                arrive(kbuf.at[:, 0, y, :, pl.ds(0, KPART)], r4.at[path, i, t])

    lanes_at = pl.ds(pl.multiple_of(block * LANES, LANES), LANES)

    @pl.when(is_worker)
    def _():
        @pl.when(served == 0)
        def _():
            arrive(bbuf.at[pl.ds(0, NSUP - 1)], lr)
            arrive(cbuf.at[pl.ds(0, NSUP - 1), pl.ds(0, 1)], cr)

        @pl.when(served == 1)
        def _():
            arrive(bbuf, lr)
            arrive(cbuf.at[:, pl.ds(0, 1)], cr)

        def client(kk, q):
            return kk * 16 + q

        def rows_of(rho):
            return pl.ds(pl.multiple_of(rho * 512, 512), 512)

        def product(rho):
            order = [(a, b) for a in range(4) for b in range(NX)]
            rhs = jnp.concatenate(
                [pn[(a * 4 + rho + WINDOW[b] + NZ) % NZ].reshape(LANES, LANES) for a, b in order], axis=0
            )
            rows = []
            for yy in range(NY):
                for h in range(2):
                    part_rows = pl.ds(h * HALF, KPART)
                    rows.append(jnp.concatenate([kbuf[a, rho, yy, b, part_rows, :] for a, b in order], axis=1))
            return jnp.dot(jnp.concatenate(rows, axis=0), rhs, preferred_element_type=F32)

        def fold(v):
            return jnp.sum(v.reshape(64, 8, LANES), axis=0)

        def total(v):
            return jnp.sum(v, axis=0, keepdims=True)

        def to_blocks(ref, rho, v):
            v = v.reshape(NY, 4, ROWS, LANES).astype(BF16)
            for yy in range(NY):
                for kk in range(4):
                    ref[kk * 4 + rho, yy] = v[yy, kk]

        zero = jnp.zeros((8, LANES), F32)

        def solve(emit, order=None):
            def first(t, c):
                rho = t
                if order is not None:
                    rho = (z + WINDOW[t] + 4) % 4
                    arrive_rows(t)
                image = product(rho)
                b = bvec[rows_of(rho), :]
                vec[rows_of(rho), :] = image
                return c[0] + fold(b * b), c[1] + fold(b * image)

            if order is None:
                norm, curve = lax.fori_loop(0, 4, first, (zero, zero))
            else:
                norm, curve = zero, zero
                for t in order:
                    norm, curve = first(t, (norm, curve))
            norm, curve = total(norm), total(curve)
            step0 = norm / curve

            def resid(rho, c):
                v = bvec[rows_of(rho), :] - step0 * vec[rows_of(rho), :]
                vec[rows_of(rho), :] = v
                return c + fold(v * v)

            norm1 = total(lax.fori_loop(0, 4, resid, zero))
            beta = norm1 / norm

            def turn(rho, c):
                v = vec[rows_of(rho), :] + beta * bvec[rows_of(rho), :]
                vec[rows_of(rho), :] = v
                to_blocks(pn, rho, v)
                return c

            lax.fori_loop(0, 4, turn, 0)

            def second(rho, c):
                return c + fold(vec[rows_of(rho), :] * product(rho))

            step1 = norm1 / total(lax.fori_loop(0, 4, second, zero))

            def finish(i, c):
                rho = (zr + i) % 4
                emit(rho, step0 * bvec[rows_of(rho), :] + step1 * vec[rows_of(rho), :])
                return c

            lax.fori_loop(0, 4, finish, 0)

        def load(s, c):
            b = bbuf[s]
            bvec[pl.ds(pl.multiple_of(((s % 16) * 4 + s // 16) * ROWS, ROWS), ROWS), :] = b
            pn[s // 4, s % 4] = b.astype(BF16)
            return c

        lax.fori_loop(0, NSUP, load, 0)

        def keep_low(rho, v):
            low[rows_of(rho), :] = v.astype(BF16)

        solve(keep_low, range(4))

        for path in range(2):
            for i in range(3):
                arrive(kbuf.at[:, :, 0, :, pl.ds(KPART, CPART)], r5.at[path, i])

        def cross_block(q):
            rho, yy = q // 4, q % 4
            blocks = []
            for zc in range(NZ):
                b = next(i for i in range(NX) if (zc - WINDOW[i] - rho) % 4 == 0)
                zz = (zc - WINDOW[b]) % NZ
                for h in range(2):
                    blocks.append(kbuf[zz // 4, rho, yy, b, h * HALF + KPART : (h + 1) * HALF, :])
            return jnp.concatenate(blocks, axis=0)

        predicted = jnp.dot(
            jnp.concatenate([cross_block(q) for q in range(16)], axis=1), low[...], preferred_element_type=F32
        )
        pred[...] = predicted.reshape(NSUP, TROWS, LANES)

        def send_pred(i, c):
            s = (sup + i) % NSUP

            @pl.when((served == 1) | (s != sup))
            def _():
                send(pred.at[s], pbuf.at[:, lanes_at], ps, pr, {"sup": s, "cls": x * 2 + served})

            return c

        lax.fori_loop(0, NSUP, send_pred, 0)

        @pl.when(served == 0)
        def _():
            pbuf[:, lanes_at] = pred[sup]

        lane = lax.broadcasted_iota(jnp.int32, (NSUP, TROWS, LANES), 2)
        row = lax.broadcasted_iota(jnp.int32, (NSUP, TROWS, LANES), 1)
        target = jnp.sum(jnp.where(lane == row, cbuf[:, 0:1, :], 0.0), axis=2, keepdims=True)
        first_class = ((x * 2 + served) * BLOCKS + block) * LANES
        onehot = jnp.where(target == (first_class + lane).astype(F32), LABEL_SCALE, 0.0)
        misfit = (predicted - onehot.reshape(NSUP * TROWS, LANES)).astype(BF16)
        for q in range(16):
            rhs = lax.dot_general(cross_block(q), misfit, (((0,), (0,)), ((), ())), preferred_element_type=F32)
            bvec[q * LANES : (q + 1) * LANES, :] = rhs
            for kk in range(4):
                pn[kk * 4 + q // 4, q % 4] = rhs[kk * ROWS : (kk + 1) * ROWS].astype(BF16)

        def keep_hyper(rho, v):
            to_blocks(hst, rho, v)

        solve(keep_hyper)

        def send_hyper(i, c):
            m = i // 4
            d = jnp.where(m % 2 == 0, 8 + m // 2, 7 - m // 2)
            zz, yy = (z + d) % NZ, (y + i + 2) % 4

            @pl.when((served == 1) | (zz != z) | (yy != y))
            def _():
                dev = {"sup": zz * NY + yy, "cls": x * 2 + served}
                send(hst.at[zz, yy], hbuf.at[:, lanes_at], hs, hr, dev)

            return c

        lax.fori_loop(0, NSUP, send_hyper, 0)

        @pl.when(served == 0)
        def _():
            hbuf[:, lanes_at] = hst[z, y]

    @pl.when((core == 0) & (kind < 3) & jnp.logical_not(is_worker))
    def _():
        for t in range(4):
            arrive_rows(t)
        for path in range(2):
            for i in range(3):
                arrive(kbuf.at[:, :, 0, :, pl.ds(KPART, CPART)], r5.at[path, i])

    def settle(buf, axis, sem, count):
        full, less = [slice(None)] * buf.ndim, [slice(None)] * buf.ndim
        less[axis] = pl.ds(0, (count - 1) * (buf.shape[axis] // count))

        @pl.when(own_worker)
        def _():
            arrive(buf.at[tuple(less)], sem)

        @pl.when(others)
        def _():
            arrive(buf.at[tuple(full)], sem)

    for t in range(3):
        arrive(ibuf.at[0, y], iws.at[t])
        arrive(tbuf.at[0, y], tws.at[t])
        arrive(jbuf.at[zq], js.at[t])
        for k in range(4):
            arrive(ibuf.at[0, y], iys.at[k, t])
            arrive(tbuf.at[0, y], tys.at[k, t])
    settle(labels, 1, ls, BLOCKS)

    @pl.when(own_worker)
    def _():
        arrive(cbuf.at[pl.ds(0, BLOCKS - 1), pl.ds(0, 1)], cs)

    @pl.when(others)
    def _():
        arrive(cbuf.at[pl.ds(0, BLOCKS), pl.ds(0, 1)], cs)

    @pl.when(core == 0)
    def _():
        arrive(part.at[pl.ds(0, NX - 1)], xs)
        arrive(kbuf.at[0, 0, 0, pl.ds(0, 3)], s1)
        arrive(kbuf.at[:, 0, 0, pl.ds(0, 3)], s6)
        for path in range(2):
            arrive(kbuf.at[:, 0, pl.ds(0, 3), :, pl.ds(0, HALF)], s2.at[path])

            def sent(count):
                arrive(kbuf.at[:, :, pl.ds(0, count), :, pl.ds(0, KPART)], s4.at[path])
                arrive(kbuf.at[:, :, pl.ds(0, count), :, pl.ds(KPART, CPART)], s5.at[path])

            pl.when(kind < 3)(functools.partial(sent, 2))
            pl.when(kind == 3)(functools.partial(sent, 3))

    @pl.when(core == 1)
    def _():
        arrive(part, xs)

    @pl.when(is_worker & (served == 0))
    def _():
        arrive(pred.at[pl.ds(0, NSUP - 1)], ps)
        arrive(low.at[pl.ds(0, (NSUP - 1) * ROWS)], hs)

    @pl.when(is_worker & (served == 1))
    def _():
        arrive(pred, ps)
        arrive(low, hs)

    settle(pbuf, 1, pr, BLOCKS)
    settle(hbuf, 1, hr, BLOCKS)


def gather_pieces(
    z, y, x, zq, zr, kind, zshift, send_labels, scales, part, rbuf, kbuf, xr, own,
    s1, r1, s2, r2, s4, r4, s5, r5, s6, r6,
):
    rbuf[own] = part[x]
    arrive(rbuf.at[pl.ds(0, 2 * NX - 1)], xr)
    summed = rbuf[0]
    for k in range(1, 2 * NX):
        summed = summed + rbuf[k]
    zc = zshift(jnp.where(x < 2, x, jnp.where(x == 2, WINDOW[2], WINDOW[3])))
    col_scale = scales[pl.ds(zc, 1), :]
    lane = lax.broadcasted_iota(jnp.int32, (ROWS, LANES), 1)
    row = lax.broadcasted_iota(jnp.int32, (ROWS, LANES), 0)
    row_scales = []
    for kk in range(4):
        zz = kk * 4 + zr
        picked = jnp.where(lane == y * ROWS + row, scales[pl.ds(zz, 1), :], 0.0)
        row_scale = jnp.sum(picked, axis=1, keepdims=True)
        row_scales.append(row_scale)
        diag = zz * LANES + y * ROWS + row == zc * LANES + lane
        block = summed[kk * ROWS : (kk + 1) * ROWS] * (row_scale * col_scale) / F
        at = (kk // 2) * HALF + (kk % 2) * ROWS
        kbuf[zq, zr, y, x, at : at + ROWS] = (block + jnp.where(diag, RIDGE, 0.0)).astype(BF16)
    row_scale = jnp.concatenate(row_scales, axis=0)
    same = lax.broadcasted_iota(jnp.int32, (LANES, LANES), 0) == lax.broadcasted_iota(jnp.int32, (LANES, LANES), 1)
    cross_scale = jnp.sum(jnp.where(same, row_scale, 0.0), axis=0, keepdims=True)
    for h in range(2):
        cross = summed[LANES + h * CPART : LANES + (h + 1) * CPART] * cross_scale / F
        kbuf[zq, zr, y, x, h * HALF + KPART : (h + 1) * HALF] = cross.astype(BF16)

    pos = (y, x)

    def last_dev(path, k):
        if path == 0:
            return device(z, (y + k) % NY, x, 0)
        return device(z, y, (x + k) % NX, 0)

    def line(path, k):
        if path == 0:
            return device(z, y, (x + k) % NX, 0)
        return device(z, (y + k) % NY, x, 0)

    def rho_of(t):
        return (z + WINDOW[t] + 4) % 4

    def window_send(ref, send_sem, recv_sems, ts):
        for t in ts:
            send(ref, ref, send_sem, recv_sems.at[t - 1], device(zshift(-WINDOW[t]), y, x, 0))

    piece = kbuf.at[zq, zr, y, x]
    for i in range(1, 4):
        send(piece, piece, s1, r1.at[i - 1], device(zshift(4 * i), y, x, 0))
    window_send(piece, s6, r6, (1, 2, 3))
    for i in range(1, 4):
        arrive(piece, r1.at[i - 1])
        window_send(kbuf.at[(zq + 4 - i) % 4, zr, y, x], s6, r6, (1, 2, 3))
    def middle(t):
        for i in (1, 3, 2):
            for path in range(2):
                ref = kbuf.at[:, rho_of(t), y, x, pl.ds(path * HALF, HALF)]
                send(ref, ref, s2.at[path], r2.at[path, i - 1, t], line(path, i))

    middle(0)
    send_labels()
    for t in range(1, 4):
        arrive(kbuf.at[:, 0, y, x], r6.at[t - 1])
        middle(t)

    def last(t):
        rho = rho_of(t)
        for a in range(2):
            refs = (
                kbuf.at[pl.ds(2 * a, 2), rho, y, :, pl.ds(0, KPART)],
                kbuf.at[pl.ds(2 * a, 2), rho, :, x, pl.ds(HALF, KPART)],
            )
            for i in (1, 3, 2):

                @pl.when((kind + i) % 4 < 3)
                def _():
                    for path in range(2):
                        send(refs[path], refs[path], s4.at[path], r4.at[path, i - 1, t], last_dev(path, i))

    for t in range(4):
        for path in range(2):
            for i in range(3):
                arrive(kbuf.at[:, 0, y, x, pl.ds(0, HALF)], r2.at[path, i, t])
        last(t)
    refs = (kbuf.at[:, :, y, :, pl.ds(KPART, CPART)], kbuf.at[:, :, :, x, pl.ds(HALF + KPART, CPART)])
    for i in (1, 3, 2):

        @pl.when((kind + i) % 4 < 3)
        def _():
            for path in range(2):
                send(refs[path], refs[path], s5.at[path], r5.at[path, i - 1], last_dev(path, i))


def local(support_feats, target_feats, scales, soft_labels, target_labels):
    width = support_feats.shape[1]
    dma = pltpu.SemaphoreType.DMA
    vmem = pl.BlockSpec(memory_space=pltpu.VMEM)
    pred, hyper = pl.pallas_call(
        kernel,
        out_shape=(
            jax.ShapeDtypeStruct((TROWS, BLOCKS * LANES), F32),
            jax.ShapeDtypeStruct((ROWS, BLOCKS * LANES), BF16),
        ),
        in_specs=[pl.BlockSpec(memory_space=pl.ANY), vmem, vmem, pl.BlockSpec(memory_space=pl.ANY), pl.BlockSpec(memory_space=pltpu.SMEM)],
        out_specs=(vmem, vmem),
        scratch_shapes=[
            pltpu.VMEM((4, NY, ROWS, width), BF16),
            pltpu.VMEM((4, NY, 16, width // 2), BF16),
            pltpu.VMEM((4, ROWS, width), BF16),
            pltpu.VMEM((NX, PIECE, LANES), F32),
            pltpu.VMEM((2 * NX, PIECE, LANES), F32),
            pltpu.VMEM((4, 4, NY, NX, PIECE, LANES), BF16),
            pltpu.VMEM((8, LANES), F32),
            pltpu.VMEM((NSUP, 8, LANES), F32),
            pltpu.VMEM((NSUP, ROWS, LANES), F32),
            pltpu.VMEM((NZ, NY, ROWS, LANES), BF16),
            pltpu.VMEM((2048, LANES), F32),
            pltpu.VMEM((2048, LANES), F32),
            pltpu.VMEM((2048, LANES), BF16),
            pltpu.VMEM((NSUP, TROWS, LANES), F32),
            pltpu.VMEM((NZ, NY, ROWS, LANES), BF16),
            pltpu.VMEM((NZ, LANES), F32),
            dma((3,)), dma((3,)), dma((3,)), dma((3,)),
            dma((4, 3)), dma((4, 3)), dma((4, 3)), dma((4, 3)),
            dma((3,)), dma((3,)), dma, dma,
            dma, dma, dma, dma,
            dma, dma((3,)), dma((2,)), dma((2, 3, 4)),
            dma((2,)), dma((2, 3, 4)), dma((2,)), dma((2, 3)), dma, dma((3,)), dma,
            dma, dma, dma, dma,
        ],
        compiler_params=pltpu.CompilerParams(collective_id=0, has_side_effects=True, vmem_limit_bytes=56 * 2**20),
        name="hypergradient",
    )(support_feats, target_feats, scales.reshape(NZ, LANES), soft_labels, target_labels)
    return pred.astype(BF16), hyper.astype(F32)


def solution(mesh):
    in_specs = (P("sup", "cls"), P("sup", "cls"), P(), P("sup", "cls"), P("sup"))
    out_specs = (P("sup", "cls"), P("sup", "cls"))
    return jax.shard_map(local, mesh=mesh, in_specs=in_specs, out_specs=out_specs, check_vma=False)
```

time: 504 us -> 130 us (0.26); the launches traced: 496 us -> 129 us
  waiting for transfers between devices: 348 us -> 0 us
  Pallas kernels: 0 us -> 125 us
  starting transfers between devices: 38.3 us -> 0 us
  blocking collectives: 30.8 us -> 0 us
  matrix products: 30.1 us -> 0 us
  local copies, waits for them, and re-layouts: 27.9 us -> 0 us
  between operations: 14.7 us -> 0.64 us
    all_gather x2 -> x0, waiting for transfers between devices: 253 us -> none  [the longest x1 147 us: local(): lax.all_gather(support_feats, 'sup', axis=0, tiled=True)]
    pallas_call x0 -> x1, Pallas kernels: none -> 125 us  [local(): pl.pallas_call(kernel, out_shape=(jax.ShapeDtypeStruct((TROWS, BLOCKS * L...]
    psum x1 -> x0, waiting for transfers between devices: 75.4 us -> none  [local(): summed = lax.psum(partial_gram, 'cls')]
    all_to_all x3 -> x0, starting transfers between devices: 38.1 us -> none  [the longest x1 14.7 us: local(): lax.all_to_all(soft_labels, 'sup', split_axis=1, concat_axis=0, tiled=True)]
    unnamed x1 -> x0, blocking collectives: 30.8 us -> none
    dot_general x7 -> x0, matrix products: 30.1 us -> none  [the longest x4 21.3 us: conjugate(): jnp.dot(kernel, direction.astype(jnp.bfloat16), preferred_element_type=jn...]
    all_to_all x3 -> x0, waiting for transfers between devices: 18.1 us -> none  [the longest x1 18.1 us: local(): lax.all_to_all(hyper_cols, 'sup', split_axis=0, concat_axis=1, tiled=True)]
    unnamed x13 -> x0, local copies, waits for them, and re-layouts: 9.57 us -> none
  transfers between devices with their start and end apart: 6 -> 0, of which waited for: 4 -> 0; matrix products, arithmetic and copies ran while one was open for 6% -> 0% of each run, Pallas kernels for 0% -> 0%
where the time goes in v2:
time: 130 us; the launch traced here: 129 us
  Pallas kernels  125 us (96%)
  other arithmetic  3.18 us (2%)
    pallas_call x1, Pallas kernels, local(): pl.pallas_call(kernel, out_shape=(jax.ShapeDtypeStruct((TROWS, BLOCKS * L...  125 us
    convert_element_type x2, other arithmetic, local(): return (pred.astype(BF16), hyper.astype(F32))  3.18 us

profile of v2, /device:TPU:1, one launch (start us, length us, event | category | flops | bytes accessed | tf_op | source)
XLA Modules:
  0.0 128.8 jit_solution(5289313305094029714)
XLA Ops:
  0.6 125.0 %hypergradient.1 = (f32[8,2688]{1,0:T(8,128)}, bf16[32,2688]{1,0:T(8,128)(2,1)}) custom-call(bf16[32,1024]{1,0:T(8,128)(2,1)} %feats.1, bf16[8,1024]{1,0:T(8,128)(2,1)} %targets.1, bf16[16,128]{1,0:T(8,128)(2,1)} %bitcast.1, f32[32,2688]{1,0:T(8,128)} %labels.1, s32[8]{0:T(128)} %classes.1), custom_call_target="tpu_custom_call" | custom-call | tf_op jit(solution)/shard_map/hypergradient/pallas_call | solution.py:536
  125.6 1.5 %convert_element_type.6 = bf16[8,2688]{1,0:T(8,128)(2,1)} convert(f32[8,2688]{1,0:T(8,128)} %get-tuple-element.4) | non-fusion elementwise | flops 21504 | bytes 129024 | tf_op jit(solution)/shard_map/convert_element_type | solution.py:572
  127.1 1.7 %convert_element_type.7 = f32[32,2688]{1,0:T(8,128)} convert(bf16[32,2688]{1,0:T(8,128)(2,1)} %get-tuple-element.5) | non-fusion elementwise | flops 86016 | bytes 516096 | tf_op jit(solution)/shard_map/convert_element_type | solution.py:572

commit v3 on v2

--- a/solution.py
+++ b/solution.py
@@ -22,6 +22,7 @@
 HALF = PIECE // 2
 KPART, CPART = LANES // 2, NY * TROWS // 2
 WINDOW = (0, 1, -1, 2)
+UNROLL = 4
 F32 = jnp.float32
 BF16 = jnp.bfloat16
 
@@ -58,7 +59,7 @@
 def kernel(
     feats, targets, scales, labels, classes, pbuf, hbuf,
     ibuf, tbuf, jbuf, part, rbuf, kbuf, cstage, cbuf, bbuf, pn, bvec, vec, low, pred, hst,
-    wide, iws, iwr, tws, twr, iys, iyr, tys, tyr, js, jr, xs, xr,
+    wide, go, iws, iwr, tws, twr, iys, iyr, tys, tyr, js, jr, xs, xr,
     ls, lr, cs, cr, s1, r1, s2, r2, s4, r4, s5, r5, s6, r6, s7, ps, pr, hs, hr,
 ):
     z, y, x, core = place()
@@ -79,15 +80,15 @@
     barrier = pltpu.get_barrier_semaphore()
     for t in range(1, 4):
         signal(barrier, device(zshift(WINDOW[t]), y, x, core))
-        signal(barrier, device(zshift(4 * t), y, x, core))
         signal(barrier, device(z, (y + t) % NY, x, core))
+    signal(barrier, device(zshift(4), y, x, core))
+    signal(barrier, device(zshift(-4), y, x, core))
 
     @pl.when(core == 0)
     def _():
         for t in range(1, 4):
             signal(barrier, device(z, y, (x + t) % NX, 0))
             signal(barrier, device(z, y, (x + t) % NX, 1))
-            signal(barrier, device(zshift(4 * t), y, x, 1))
         signal(barrier, device(z, y, x, 1))
 
     own_window = pltpu.make_async_copy(feats, ibuf.at[0, y], s7)
@@ -106,7 +107,7 @@
 
     own_window.wait()
     own_stride.wait()
-    pl.semaphore_wait(barrier, 3 * 4 + 4 * core)
+    pl.semaphore_wait(barrier, 3 * 3 + 2 + core)
 
     def spread(t, i):
         dev = device(z, (y + i) % NY, x, core)
@@ -118,15 +119,31 @@
         send(ibuf.at[0, y], ibuf.at[t, y], iws.at[t - 1], iwr.at[t - 1], dev)
         send(tbuf.at[0, y], tbuf.at[t, y], tws.at[t - 1], twr.at[t - 1], dev)
         spread(0, t)
-    for i in (2, 1, 3):
+
+    def stride_send(i):
         send(jbuf.at[zq], jbuf.at[zq], js.at[i - 1], jr.at[i - 1], device(zshift(4 * i), y, x, core))
-    for t in range(1, 4):
+
+    stride_send(1)
+    stride_send(3)
+
+    def window_in(t):
         arrive(ibuf.at[t, y], iwr.at[t - 1])
         arrive(tbuf.at[t, y], twr.at[t - 1])
         for i in range(1, 4):
             spread(t, i)
-    for i in range(3):
+
+    def stride_on(i, slot, start, to):
         arrive(jbuf.at[zq], jr.at[i])
+        ref = jbuf.at[slot % 4, pl.ds(start, ROWS // 2)]
+        send(ref, ref, js.at[i + 1], jr.at[i + 1], device(zshift(to), y, x, core))
+
+    window_in(1)
+    window_in(2)
+    stride_on(0, zq + 3, 0, 4)
+    stride_on(2, zq + 1, ROWS // 2, -4)
+    window_in(3)
+    arrive(jbuf.at[zq, pl.ds(0, ROWS // 2)], jr.at[1])
+    arrive(jbuf.at[zq, pl.ds(0, ROWS // 2)], jr.at[3])
     for t in range(4):
         for i in range(3):
             arrive(ibuf.at[t, y], iyr.at[t, i])
@@ -162,9 +179,12 @@
         return c
 
     def send_labels():
-        lax.fori_loop(0, BLOCKS, send_label, 0)
-
-    pl.when(core == 1)(send_labels)
+        lax.fori_loop(0, BLOCKS, send_label, 0, unroll=3)
+
+    @pl.when(core == 1)
+    def _():
+        pl.semaphore_wait(go, 1)
+        send_labels()
 
     @pl.when(own_worker)
     def _():
@@ -178,7 +198,7 @@
     @pl.when(core == 0)
     def _():
         gather_pieces(
-            z, y, x, zq, zr, kind, zshift, send_labels, wide, part, rbuf, kbuf, xr, own,
+            z, y, x, zq, zr, kind, zshift, send_labels, go, wide, part, rbuf, kbuf, xr, own,
             s1, r1, s2, r2, s4, r4, s5, r5, s6, r6,
         )
 
@@ -322,7 +342,7 @@
 
             return c
 
-        lax.fori_loop(0, NSUP, send_pred, 0)
+        lax.fori_loop(0, NSUP, send_pred, 0, unroll=UNROLL)
 
         @pl.when(served == 0)
         def _():
@@ -357,7 +377,7 @@
 
             return c
 
-        lax.fori_loop(0, NSUP, send_hyper, 0)
+        lax.fori_loop(0, NSUP, send_hyper, 0, unroll=UNROLL)
 
         @pl.when(served == 0)
         def _():
@@ -386,10 +406,12 @@
     for t in range(3):
         arrive(ibuf.at[0, y], iws.at[t])
         arrive(tbuf.at[0, y], tws.at[t])
-        arrive(jbuf.at[zq], js.at[t])
         for k in range(4):
             arrive(ibuf.at[0, y], iys.at[k, t])
             arrive(tbuf.at[0, y], tys.at[k, t])
+    for i in range(2):
+        arrive(jbuf.at[zq], js.at[2 * i])
+        arrive(jbuf.at[zq, pl.ds(0, ROWS // 2)], js.at[2 * i + 1])
     settle(labels, 1, ls, BLOCKS)
 
     @pl.when(own_worker)
@@ -434,7 +456,7 @@
 
 
 def gather_pieces(
-    z, y, x, zq, zr, kind, zshift, send_labels, scales, part, rbuf, kbuf, xr, own,
+    z, y, x, zq, zr, kind, zshift, send_labels, go, scales, part, rbuf, kbuf, xr, own,
     s1, r1, s2, r2, s4, r4, s5, r5, s6, r6,
 ):
     rbuf[own] = part[x]
@@ -496,10 +518,10 @@
                 send(ref, ref, s2.at[path], r2.at[path, i - 1, t], line(path, i))
 
     middle(0)
-    send_labels()
     for t in range(1, 4):
         arrive(kbuf.at[:, 0, y, x], r6.at[t - 1])
         middle(t)
+    signal(go, device(z, y, x, 1))
 
     def last(t):
         rho = rho_of(t)
@@ -520,6 +542,8 @@
             for i in range(3):
                 arrive(kbuf.at[:, 0, y, x, pl.ds(0, HALF)], r2.at[path, i, t])
         last(t)
+        if t == 0:
+            send_labels()
     refs = (kbuf.at[:, :, y, :, pl.ds(KPART, CPART)], kbuf.at[:, :, :, x, pl.ds(HALF + KPART, CPART)])
     for i in (1, 3, 2):
 
@@ -558,9 +582,10 @@
             pltpu.VMEM((NSUP, TROWS, LANES), F32),
             pltpu.VMEM((NZ, NY, ROWS, LANES), BF16),
             pltpu.VMEM((NZ, LANES), F32),
+            pltpu.SemaphoreType.REGULAR,
             dma((3,)), dma((3,)), dma((3,)), dma((3,)),
             dma((4, 3)), dma((4, 3)), dma((4, 3)), dma((4, 3)),
-            dma((3,)), dma((3,)), dma, dma,
+            dma((4,)), dma((4,)), dma, dma,
             dma, dma, dma, dma,
             dma, dma((3,)), dma((2,)), dma((2, 3, 4)),
             dma((2,)), dma((2, 3, 4)), dma((2,)), dma((2, 3)), dma, dma((3,)), dma,

time: 130 us -> 127 us (0.977)
  Pallas kernels: 125 us -> 121 us
    pallas_call x1, Pallas kernels: 125 us -> 121 us  [local(): pl.pallas_call(kernel, out_shape=(jax.ShapeDtypeStruct((TROWS, BLOCKS * L...]
where the time goes in v3:
time: 127 us; the launch traced here: 125 us
  Pallas kernels  121 us (95%)
  other arithmetic  3.18 us (3%)
    pallas_call x1, Pallas kernels, local(): pl.pallas_call(kernel, out_shape=(jax.ShapeDtypeStruct((TROWS, BLOCKS * L...  121 us
    convert_element_type x2, other arithmetic, local(): return (pred.astype(BF16), hyper.astype(F32))  3.18 us

profile of v3, /device:TPU:1, one launch (start us, length us, event | category | flops | bytes accessed | tf_op | source)
XLA Modules:
  0.0 125.0 jit_solution(265284528285903499)
XLA Ops:
  0.6 121.2 %hypergradient.1 = (f32[8,2688]{1,0:T(8,128)}, bf16[32,2688]{1,0:T(8,128)(2,1)}) custom-call(bf16[32,1024]{1,0:T(8,128)(2,1)} %feats.1, bf16[8,1024]{1,0:T(8,128)(2,1)} %targets.1, bf16[16,128]{1,0:T(8,128)(2,1)} %bitcast.1, f32[32,2688]{1,0:T(8,128)} %labels.1, s32[8]{0:T(128)} %classes.1), custom_call_target="tpu_custom_call" | custom-call | tf_op jit(solution)/shard_map/hypergradient/pallas_call | solution.py:560
  121.9 1.5 %convert_element_type.6 = bf16[8,2688]{1,0:T(8,128)(2,1)} convert(f32[8,2688]{1,0:T(8,128)} %get-tuple-element.4) | non-fusion elementwise | flops 21504 | bytes 129024 | tf_op jit(solution)/shard_map/convert_element_type | solution.py:597
  123.4 1.7 %convert_element_type.7 = f32[32,2688]{1,0:T(8,128)} convert(bf16[32,2688]{1,0:T(8,128)(2,1)} %get-tuple-element.5) | non-fusion elementwise | flops 86016 | bytes 516096 | tf_op jit(solution)/shard_map/convert_element_type | solution.py:597

commit v4 on v3

--- a/solution.py
+++ b/solution.py
@@ -23,6 +23,8 @@
 KPART, CPART = LANES // 2, NY * TROWS // 2
 WINDOW = (0, 1, -1, 2)
 UNROLL = 4
+SPLIT = 2
+LABELS_AFTER = 3
 F32 = jnp.float32
 BF16 = jnp.bfloat16
 
@@ -505,10 +507,10 @@
             send(ref, ref, send_sem, recv_sems.at[t - 1], device(zshift(-WINDOW[t]), y, x, 0))
 
     piece = kbuf.at[zq, zr, y, x]
-    for i in range(1, 4):
+    for i in (2, 1, 3):
         send(piece, piece, s1, r1.at[i - 1], device(zshift(4 * i), y, x, 0))
     window_send(piece, s6, r6, (1, 2, 3))
-    for i in range(1, 4):
+    for i in (1, 3, 2):
         arrive(piece, r1.at[i - 1])
         window_send(kbuf.at[(zq + 4 - i) % 4, zr, y, x], s6, r6, (1, 2, 3))
     def middle(t):
@@ -517,18 +519,20 @@
                 ref = kbuf.at[:, rho_of(t), y, x, pl.ds(path * HALF, HALF)]
                 send(ref, ref, s2.at[path], r2.at[path, i - 1, t], line(path, i))
 
-    middle(0)
-    for t in range(1, 4):
-        arrive(kbuf.at[:, 0, y, x], r6.at[t - 1])
+    for t in range(4):
+        if t > 0:
+            arrive(kbuf.at[:, 0, y, x], r6.at[t - 1])
         middle(t)
-    signal(go, device(z, y, x, 1))
+        if t == LABELS_AFTER:
+            signal(go, device(z, y, x, 1))
+            send_labels()
 
     def last(t):
         rho = rho_of(t)
-        for a in range(2):
+        for a in range(4 // SPLIT):
             refs = (
-                kbuf.at[pl.ds(2 * a, 2), rho, y, :, pl.ds(0, KPART)],
-                kbuf.at[pl.ds(2 * a, 2), rho, :, x, pl.ds(HALF, KPART)],
+                kbuf.at[pl.ds(SPLIT * a, SPLIT), rho, y, :, pl.ds(0, KPART)],
+                kbuf.at[pl.ds(SPLIT * a, SPLIT), rho, :, x, pl.ds(HALF, KPART)],
             )
             for i in (1, 3, 2):
 
@@ -542,8 +546,6 @@
             for i in range(3):
                 arrive(kbuf.at[:, 0, y, x, pl.ds(0, HALF)], r2.at[path, i, t])
         last(t)
-        if t == 0:
-            send_labels()
     refs = (kbuf.at[:, :, y, :, pl.ds(KPART, CPART)], kbuf.at[:, :, :, x, pl.ds(HALF + KPART, CPART)])
     for i in (1, 3, 2):
 

time: 127 us -> 126 us (level); the launches traced: 125 us -> 126 us
  no operation moved by 1% of the time
where the time goes in v4:
time: 126 us
  Pallas kernels  122 us (97%)
  other arithmetic  3.18 us (3%)
    pallas_call x1, Pallas kernels, local(): pl.pallas_call(kernel, out_shape=(jax.ShapeDtypeStruct((TROWS, BLOCKS * L...  122 us
    convert_element_type x2, other arithmetic, local(): return (pred.astype(BF16), hyper.astype(F32))  3.18 us

profile of v4, /device:TPU:1, one launch (start us, length us, event | category | flops | bytes accessed | tf_op | source)
XLA Modules:
  0.0 125.7 jit_solution(16063502121642649361)
XLA Ops:
  0.6 121.9 %hypergradient.1 = (f32[8,2688]{1,0:T(8,128)}, bf16[32,2688]{1,0:T(8,128)(2,1)}) custom-call(bf16[32,1024]{1,0:T(8,128)(2,1)} %feats.1, bf16[8,1024]{1,0:T(8,128)(2,1)} %targets.1, bf16[16,128]{1,0:T(8,128)(2,1)} %bitcast.1, f32[32,2688]{1,0:T(8,128)} %labels.1, s32[8]{0:T(128)} %classes.1), custom_call_target="tpu_custom_call" | custom-call | tf_op jit(solution)/shard_map/hypergradient/pallas_call | solution.py:562
  122.5 1.5 %convert_element_type.6 = bf16[8,2688]{1,0:T(8,128)(2,1)} convert(f32[8,2688]{1,0:T(8,128)} %get-tuple-element.4) | non-fusion elementwise | flops 21504 | bytes 129024 | tf_op jit(solution)/shard_map/convert_element_type | solution.py:599
  124.0 1.7 %convert_element_type.7 = f32[32,2688]{1,0:T(8,128)} convert(bf16[32,2688]{1,0:T(8,128)(2,1)} %get-tuple-element.5) | non-fusion elementwise | flops 86016 | bytes 516096 | tf_op jit(solution)/shard_map/convert_element_type | solution.py:599
